TPU v7x, 32 devices: a whole 2x2x4 slice. The times are simulated.
32 devices in a mesh: seq: 8 (over z, y), head: 4 (over x, core).
Axes of the slice: x: 2, y: 2, z: 4, core: 2. Of those that a mesh axis runs over, the one named last changes fastest.
Arguments:
- queries: bfloat16 [2048, 4096], P('seq', 'head'), may hold values from -32 to 32
- key_rows: bfloat16 [2048, 4096], P('seq', 'head'), may hold values from -6 to 6
- value_rows: bfloat16 [2048, 4096], P('seq', 'head'), may hold values from -6 to 6
- out_weight: bfloat16 [4096, 4096], P('head', 'seq'), may hold values from -0.125 to 0.125
- grad_output: bfloat16 [2048, 4096], P('seq', 'head'), may hold values from -6 to 6
- cluster_ids: int32 [2048], P('seq'), may hold values from 0 to 7, as said below
- block_pattern: int32 [8, 2, 2], replicated, may hold values from 0 to 1, as said below
Outputs:
- layer_out: bfloat16 [2048, 4096], P('seq', 'head')
- grad_queries: bfloat16 [2048, 4096], P('seq', 'head')
- grad_keys: bfloat16 [2048, 4096], P('seq', 'head')
- grad_values: bfloat16 [2048, 4096], P('seq', 'head')
Inputs may be any that keep to these rules, and one draw needn't show every extreme that they name: `cluster_ids`: every cluster holds exactly 256 tokens. The 256 tokens of one index of seq name one cluster at most 64 times, and each such index names some cluster exactly 64 times. block_pattern[c, b, b] = 1 and block_pattern[c, b, b2] = 0 for b2 > b.
All inputs are finite; a program needn't handle non-finite values.
Results may differ from a plain program's by a relative error of at most 0.03.
Values may be sent and summed in bfloat16 or wider, within the bound.
A program may use at most 64 MiB of HBM per device.

v0:
```python
import math

import jax
import jax.numpy as jnp
from jax import lax
from jax.sharding import PartitionSpec as P

HD = 128
BLK = 128


def probabilities(query_part, key_part, allowed, score_scale):
    scores = (
        jnp.einsum("qd,kd->qk", query_part, key_part, preferred_element_type=jnp.float32)
        * score_scale
    )
    scores = jnp.where(allowed, scores, -jnp.inf)
    shifted = jnp.exp(scores - jnp.max(scores, axis=1, keepdims=True))
    return shifted / jnp.sum(shifted, axis=1, keepdims=True)


def attend(query_side, key_side, value_side, allowed, head_count, score_scale):
    results = []
    for which_head in range(head_count):
        lower = which_head * HD
        probs = probabilities(
            query_side[:, lower : lower + HD], key_side[:, lower : lower + HD], allowed, score_scale
        )
        mixed = jnp.dot(
            probs.astype(jnp.bfloat16),
            value_side[:, lower : lower + HD],
            preferred_element_type=jnp.float32,
        )
        results.append(mixed.astype(jnp.bfloat16))
    return jnp.concatenate(results, axis=1)


def attend_back(
    query_side, key_side, value_side, allowed, attn_side, grad_side, head_count, score_scale
):
    grad_q, grad_k, grad_v = ([], [], [])
    for which_head in range(head_count):
        lower = which_head * HD
        query_head = query_side[:, lower : lower + HD]
        key_head = key_side[:, lower : lower + HD]
        value_head = value_side[:, lower : lower + HD]
        grad_head = grad_side[:, lower : lower + HD]
        attn_head = attn_side[:, lower : lower + HD]
        probs = probabilities(query_head, key_head, allowed, score_scale)
        probs_low = probs.astype(jnp.bfloat16)
        delta = jnp.sum(
            grad_head.astype(jnp.float32) * attn_head.astype(jnp.float32), axis=1, keepdims=True
        )
        dprobs = jnp.einsum("qd,kd->qk", grad_head, value_head, preferred_element_type=jnp.float32)
        dscores = (probs * (dprobs - delta)).astype(jnp.bfloat16)
        grad_q.append(
            (jnp.dot(dscores, key_head, preferred_element_type=jnp.float32) * score_scale).astype(
                jnp.bfloat16
            )
        )
        grad_k.append(
            (
                jnp.einsum("qk,qd->kd", dscores, query_head, preferred_element_type=jnp.float32)
                * score_scale
            ).astype(jnp.bfloat16)
        )
        grad_v.append(
            jnp.einsum(
                "qk,qd->kd", probs_low, grad_head, preferred_element_type=jnp.float32
            ).astype(jnp.bfloat16)
        )
    return (
        jnp.concatenate(grad_q, axis=1),
        jnp.concatenate(grad_k, axis=1),
        jnp.concatenate(grad_v, axis=1),
    )


def on_device(queries, key_rows, value_rows, out_weight, grad_output, cluster_ids, block_pattern):
    tokens = queries.shape[0]
    width = queries.shape[1]
    head_count = width // HD
    groups = lax.axis_size("seq")
    slot_rows = 2 * tokens // groups
    slot_total = groups * slot_rows
    blocks = block_pattern.shape[1]
    owner_index = lax.axis_index("seq")
    score_scale = 1.0 / math.sqrt(HD)
    members = (cluster_ids[:, None] == jnp.arange(groups, dtype=jnp.int32)[None, :]).astype(
        jnp.int32
    )
    earlier = jnp.cumsum(members, axis=0) - members
    local_rank = jnp.sum(earlier * members, axis=1)
    send_counts = jnp.sum(members, axis=0)
    slot_index = cluster_ids * slot_rows + local_rank

    def to_slots(row_data):
        return (
            jnp.zeros((slot_total, row_data.shape[1]), row_data.dtype).at[slot_index].set(row_data)
        )

    def from_slots(buffer):
        return jnp.take(buffer, slot_index, axis=0)

    full_weight = lax.all_gather(out_weight, "seq", axis=1, tiled=True)
    query_in, key_in, value_in, got_counts = (
        lax.all_to_all(to_slots(queries), "seq", split_axis=0, concat_axis=0, tiled=True),
        lax.all_to_all(to_slots(key_rows), "seq", split_axis=0, concat_axis=0, tiled=True),
        lax.all_to_all(to_slots(value_rows), "seq", split_axis=0, concat_axis=0, tiled=True),
        lax.all_to_all(send_counts, "seq", split_axis=0, concat_axis=0, tiled=True),
    )
    offsets = jnp.cumsum(got_counts) - got_counts
    pattern = lax.dynamic_index_in_dim(block_pattern, owner_index, 0, keepdims=False).astype(
        jnp.float32
    )
    slot_source = jnp.arange(slot_total, dtype=jnp.int32) // slot_rows
    slot_place = jnp.arange(slot_total, dtype=jnp.int32) % slot_rows
    row_live = slot_place < jnp.take(got_counts, slot_source)
    rank_rows = jnp.take(offsets, slot_source) + slot_place
    query_side, key_side, value_side = (query_in, key_in, value_in)
    onehot = (rank_rows[:, None] // BLK == jnp.arange(blocks, dtype=jnp.int32)[None, :]).astype(
        jnp.float32
    )
    block_ok = jnp.dot(jnp.dot(onehot, pattern), onehot.T) > 0.5
    usable = (
        block_ok
        & (rank_rows[None, :] <= rank_rows[:, None])
        & row_live[None, :]
        & row_live[:, None]
    )
    diagonal = jnp.eye(rank_rows.shape[0], dtype=bool)
    allowed = usable | diagonal & ~row_live[:, None]
    attn_side = attend(query_side, key_side, value_side, allowed, head_count, score_scale)
    attn_local = from_slots(
        lax.all_to_all(attn_side, "seq", split_axis=0, concat_axis=0, tiled=True)
    )
    partial_value = jnp.dot(attn_local, full_weight, preferred_element_type=jnp.float32)
    rounded_part = lax.optimization_barrier(partial_value.astype(jnp.bfloat16)).astype(jnp.float32)
    layer_out = lax.psum_scatter(
        rounded_part.astype(jnp.bfloat16), "head", scatter_dimension=1, tiled=True
    )
    grad_sum = jnp.einsum(
        "td,wd->tw",
        lax.all_gather(grad_output, "head", axis=1, tiled=True),
        full_weight,
        preferred_element_type=jnp.float32,
    )
    grad_attention = grad_sum.astype(jnp.bfloat16)
    grad_in = lax.all_to_all(
        to_slots(grad_attention), "seq", split_axis=0, concat_axis=0, tiled=True
    )
    grad_q, grad_k, grad_v = attend_back(
        query_side, key_side, value_side, allowed, attn_side, grad_in, head_count, score_scale
    )
    back_q, back_k, back_v = (
        lax.all_to_all(grad_q, "seq", split_axis=0, concat_axis=0, tiled=True),
        lax.all_to_all(grad_k, "seq", split_axis=0, concat_axis=0, tiled=True),
        lax.all_to_all(grad_v, "seq", split_axis=0, concat_axis=0, tiled=True),
    )
    return (layer_out, from_slots(back_q), from_slots(back_k), from_slots(back_v))


def solution(mesh):
    in_specs = (
        P("seq", "head"),
        P("seq", "head"),
        P("seq", "head"),
        P("head", "seq"),
        P("seq", "head"),
        P("seq"),
        P(),
    )
    out_specs = (P("seq", "head"), P("seq", "head"), P("seq", "head"), P("seq", "head"))
    return jax.shard_map(
        on_device, mesh=mesh, in_specs=in_specs, out_specs=out_specs, check_vma=False
    )
```

profile of v0, /device:TPU:28, one launch (start us, length us, event | category | flops | bytes accessed | tf_op | source)
XLA Modules:
  0.0 405.4 jit_solution(12948294410906341447)
XLA Ops:
  11.7 6.0 %all-to-all-start = ((s32[8,1,1]{2,1,0:T(1,128)}), s32[8,1,1]{2,1,0:T(1,128)S(1)}, u32[]{:S(2)}, u32[]{:S(2)}) async-start(s32[8,1,1]{2,1,0:T(1,128)} %copy.64), calls=%async_computation | async-start | bytes 8192 | tf_op jit(solution)/shard_map/all_to_all | solution.py:110
  18.9 3.1 scatter_custom_fusion
  22.1 6.0 %all-to-all-start.1 = ((bf16[8,64,1024]{2,1,0:T(8,128)(2,1)}), bf16[8,64,1024]{2,1,0:T(8,128)(2,1)S(1)}, u32[]{:S(2)}, u32[]{:S(2)}) async-start(bf16[8,64,1024]{2,1,0:T(8,128)(2,1)} %bitcast.21), calls=%async_computation.1 | async-start | bytes 2097152 | tf_op jit(solution)/shard_map/all_to_all | solution.py:107
  28.1 3.2 scatter_custom_fusion.1
  31.2 36.3 %all-to-all-done.1 = bf16[8,64,1024]{2,1,0:T(8,128)(2,1)S(1)} async-done(((bf16[8,64,1024]{2,1,0:T(8,128)(2,1)}), bf16[8,64,1024]{2,1,0:T(8,128)(2,1)S(1)}, u32[]{:S(2)}, u32[]{:S(2)}) %all-to-all-start.1) | async-done | bytes 1048608 | tf_op jit(solution)/shard_map/all_to_all | solution.py:107
  67.5 7.3 %all-to-all-start.2 = ((bf16[8,64,1024]{2,1,0:T(8,128)(2,1)}), bf16[8,64,1024]{2,1,0:T(8,128)(2,1)S(1)}, u32[]{:S(2)}, u32[]{:S(2)}) async-start(bf16[8,64,1024]{2,1,0:T(8,128)(2,1)} %bitcast.23), calls=%async_computation.2 | async-start | bytes 2097152 | tf_op jit(solution)/shard_map/all_to_all | solution.py:108
  74.8 3.2 scatter_custom_fusion.2
  79.2 5.0 %fusion.185 = (pred[512]{0:T(512)(128)(4,1)S(1)}, pred[512]{0:T(512)(128)(4,1)S(1)}) fusion(s32[]{:T(128)} %bitcast.20, s32[]{:T(128)} %bitcast.19, s32[]{:T(128)} %bitcast.18, s32[]{:T(128)} %bitcast.17, s32[]{:T(128)} %bitcast.16, s32[]{:T(128)} %bitcast.15, s32[]{:T(128)} %bitcast.14, s32[]{:T(128)} %bitcast.13), kind=kLoop, calls=%fused_computation.301 | loop fusion | flops 17920 | bytes 1056 | tf_op jit(solution)/shard_map/not | solution.py:132
  85.0 5.0 %add_select_fusion = (s32[512]{0:T(512)S(1)}, s32[512]{0:T(512)S(1)}) fusion(s32[]{:T(128)} %bitcast.12, s32[]{:T(128)} %bitcast.11, s32[]{:T(128)} %bitcast.10, s32[]{:T(128)} %bitcast.9, s32[]{:T(128)} %bitcast.8, s32[]{:T(128)} %bitcast.7, s32[]{:T(128)} %bitcast.6, s32[]{:T(128)} %bitcast.5), kind=kLoop, calls=%fused_computation.260 | loop fusion | flops 25088 | bytes 4128 | tf_op jit(solution)/shard_map/jit(floor_divide)/jit(_where)/select_n | solution.py:121
  90.7 17.4 %all-to-all-done.2 = bf16[8,64,1024]{2,1,0:T(8,128)(2,1)S(1)} async-done(((bf16[8,64,1024]{2,1,0:T(8,128)(2,1)}), bf16[8,64,1024]{2,1,0:T(8,128)(2,1)S(1)}, u32[]{:S(2)}, u32[]{:S(2)}) %all-to-all-start.2) | async-done | bytes 1048608 | tf_op jit(solution)/shard_map/all_to_all | solution.py:108
  108.1 6.6 %all-to-all-start.3 = ((bf16[8,64,1024]{2,1,0:T(8,128)(2,1)}), bf16[8,64,1024]{2,1,0:T(8,128)(2,1)}, u32[]{:S(2)}, u32[]{:S(2)}) async-start(bf16[8,64,1024]{2,1,0:T(8,128)(2,1)} %bitcast.25), calls=%async_computation.3 | async-start | bytes 2097152 | tf_op jit(solution)/shard_map/all_to_all | solution.py:109
  121.9 47.3 %all-to-all-done.3 = bf16[8,64,1024]{2,1,0:T(8,128)(2,1)} async-done(((bf16[8,64,1024]{2,1,0:T(8,128)(2,1)}), bf16[8,64,1024]{2,1,0:T(8,128)(2,1)}, u32[]{:S(2)}, u32[]{:S(2)}) %all-to-all-start.3) | async-done | bytes 1048608 | tf_op jit(solution)/shard_map/all_to_all | solution.py:109
  192.6 7.3 %all-to-all-start.4 = ((bf16[8,64,1024]{2,1,0:T(8,128)(2,1)}), bf16[8,64,1024]{2,1,0:T(8,128)(2,1)S(1)}, u32[]{:S(2)}, u32[]{:S(2)}) async-start(bf16[8,64,1024]{2,1,0:T(8,128)(2,1)} %bitcast.27), calls=%async_computation.4 | async-start | bytes 2097152 | tf_op jit(solution)/shard_map/all_to_all | solution.py:135
  199.8 19.6 %all-gather.3.cloned.1.call-done = bf16[1024,4096]{1,0:T(8,128)(2,1)} async-done(((bf16[1024,512]{1,0:T(8,128)(2,1)}), bf16[1024,4096]{1,0:T(8,128)(2,1)}) %all-gather.3.cloned.1.call-update) | async-done | bytes 8388624 | tf_op jit(solution)/shard_map/all_gather | solution.py:105
  219.4 6.4 %convolution_convert_fusion.1 = bf16[256,1024]{1,0:T(8,128)(2,1)S(1)} fusion(bf16[256,4096]{1,0:T(8,128)(2,1)} %all-gather.5.cloned.1.call-done, bf16[1024,4096]{1,0:T(8,128)(2,1)} %all-gather.3.cloned.1.call-done), kind=kOutput, calls=%fused_computation.41 | convolution fusion | flops 2147745792 | bytes 11010048 | tf_op jit(solution)/shard_map/td,wd->tw/dot_general | solution.py:142
  228.5 6.0 %all-to-all-start.5 = ((bf16[8,64,1024]{2,1,0:T(8,128)(2,1)}), bf16[8,64,1024]{2,1,0:T(8,128)(2,1)S(1)}, u32[]{:S(2)}, u32[]{:S(2)}) async-start(bf16[8,64,1024]{2,1,0:T(8,128)(2,1)} %bitcast.132), calls=%async_computation.6 | async-start | bytes 2097152 | tf_op jit(solution)/shard_map/all_to_all | solution.py:149
  236.5 7.4 %convolution_convert_fusion = bf16[256,4096]{1,0:T(8,128)(2,1)} fusion(bf16[1024,4096]{1,0:T(8,128)(2,1)} %all-gather.3.cloned.1.call-done, bf16[256,1024]{1,0:T(8,128)(2,1)} %gather_fusion, pred[256]{0:T(512)(128)(4,1)S(1)} %copy-done.47), kind=kOutput, calls=%fused_computation.8 | convolution fusion | flops 2148794368 | bytes 11010304 | tf_op jit(solution)/shard_map/dot_general | solution.py:137
  243.9 12.9 %all-to-all-done.5 = bf16[8,64,1024]{2,1,0:T(8,128)(2,1)S(1)} async-done(((bf16[8,64,1024]{2,1,0:T(8,128)(2,1)}), bf16[8,64,1024]{2,1,0:T(8,128)(2,1)S(1)}, u32[]{:S(2)}, u32[]{:S(2)}) %all-to-all-start.5) | async-done | bytes 1048608 | tf_op jit(solution)/shard_map/all_to_all | solution.py:149
  307.7 6.1 %all-to-all-start.7 = ((bf16[8,64,1024]{2,1,0:T(8,128)(2,1)}), bf16[8,64,1024]{2,1,0:T(8,128)(2,1)S(1)}, u32[]{:S(2)}, u32[]{:S(2)}) async-start(bf16[8,64,1024]{2,1,0:T(8,128)(2,1)} %bitcast.131), calls=%async_computation.8 | async-start | bytes 2097152 | tf_op jit(solution)/shard_map/all_to_all | solution.py:157
  331.8 5.3 %all-to-all-done.7 = bf16[8,64,1024]{2,1,0:T(8,128)(2,1)S(1)} async-done(((bf16[8,64,1024]{2,1,0:T(8,128)(2,1)}), bf16[8,64,1024]{2,1,0:T(8,128)(2,1)S(1)}, u32[]{:S(2)}, u32[]{:S(2)}) %all-to-all-start.7) | async-done | bytes 1048608 | tf_op jit(solution)/shard_map/all_to_all | solution.py:157
  337.1 6.0 %all-to-all-start.6 = ((bf16[8,64,1024]{2,1,0:T(8,128)(2,1)}), bf16[8,64,1024]{2,1,0:T(8,128)(2,1)S(1)}, u32[]{:S(2)}, u32[]{:S(2)}) async-start(bf16[8,64,1024]{2,1,0:T(8,128)(2,1)} %bitcast.130), calls=%async_computation.7 | async-start | bytes 2097152 | tf_op jit(solution)/shard_map/all_to_all | solution.py:156
  361.4 5.3 %all-to-all-done.6 = bf16[8,64,1024]{2,1,0:T(8,128)(2,1)S(1)} async-done(((bf16[8,64,1024]{2,1,0:T(8,128)(2,1)}), bf16[8,64,1024]{2,1,0:T(8,128)(2,1)S(1)}, u32[]{:S(2)}, u32[]{:S(2)}) %all-to-all-start.6) | async-done | bytes 1048608 | tf_op jit(solution)/shard_map/all_to_all | solution.py:156
  366.7 6.0 %all-to-all-start.8 = ((bf16[8,64,1024]{2,1,0:T(8,128)(2,1)}), bf16[8,64,1024]{2,1,0:T(8,128)(2,1)S(1)}, u32[]{:S(2)}, u32[]{:S(2)}) async-start(bf16[8,64,1024]{2,1,0:T(8,128)(2,1)} %bitcast.133), calls=%async_computation.9 | async-start | bytes 2097152 | tf_op jit(solution)/shard_map/all_to_all | solution.py:158
  375.9 20.5 %all-to-all-done.8 = bf16[8,64,1024]{2,1,0:T(8,128)(2,1)S(1)} async-done(((bf16[8,64,1024]{2,1,0:T(8,128)(2,1)}), bf16[8,64,1024]{2,1,0:T(8,128)(2,1)S(1)}, u32[]{:S(2)}, u32[]{:S(2)}) %all-to-all-start.8) | async-done | bytes 1048608 | tf_op jit(solution)/shard_map/all_to_all | solution.py:158
  (215 shorter events, 136.0 us)
Async XLA Ops:
  7.2 70.8 %copy-start.46 = (s32[8,2,2]{0,2,1:T(2,128)S(1)}, s32[8,2,2]{0,2,1:T(2,128)}, u32[]{:S(2)}) copy-start(s32[8,2,2]{0,2,1:T(2,128)} %param.17) | copy-start | bytes 388
  7.2 192.7 %all-gather.5.cloned.1.call-start = ((), (), s32[]{:S(2)}) async-start(), calls=%async_computation.12 | async-start | bytes 2621440 | tf_op jit(solution)/shard_map/all_gather | solution.py:144
  7.9 211.5 %all-gather.3.cloned.1.call-start = ((), (), s32[]{:S(2)}) async-start(), calls=%async_computation.10 | async-start | bytes 9437184 | tf_op jit(solution)/shard_map/all_gather | solution.py:105
  11.7 10.3 %all-to-all-start = ((s32[8,1,1]{2,1,0:T(1,128)}), s32[8,1,1]{2,1,0:T(1,128)S(1)}, u32[]{:S(2)}, u32[]{:S(2)}) async-start(s32[8,1,1]{2,1,0:T(1,128)} %copy.64), calls=%async_computation | async-start | bytes 8192 | tf_op jit(solution)/shard_map/all_to_all | solution.py:110
  18.9 59.0 %copy-start.44 = (s32[256]{0:T(256)}, s32[256]{0:T(256)S(1)}, u32[]{:S(2)}) copy-start(s32[256]{0:T(256)S(1)} %get-tuple-element.9) | copy-start | bytes 3076
  22.1 45.5 %all-to-all-start.1 = ((bf16[8,64,1024]{2,1,0:T(8,128)(2,1)}), bf16[8,64,1024]{2,1,0:T(8,128)(2,1)S(1)}, u32[]{:S(2)}, u32[]{:S(2)}) async-start(bf16[8,64,1024]{2,1,0:T(8,128)(2,1)} %bitcast.21), calls=%async_computation.1 | async-start | bytes 2097152 | tf_op jit(solution)/shard_map/all_to_all | solution.py:107
  67.5 40.6 %all-to-all-start.2 = ((bf16[8,64,1024]{2,1,0:T(8,128)(2,1)}), bf16[8,64,1024]{2,1,0:T(8,128)(2,1)S(1)}, u32[]{:S(2)}, u32[]{:S(2)}) async-start(bf16[8,64,1024]{2,1,0:T(8,128)(2,1)} %bitcast.23), calls=%async_computation.2 | async-start | bytes 2097152 | tf_op jit(solution)/shard_map/all_to_all | solution.py:108
  108.1 61.1 %all-to-all-start.3 = ((bf16[8,64,1024]{2,1,0:T(8,128)(2,1)}), bf16[8,64,1024]{2,1,0:T(8,128)(2,1)}, u32[]{:S(2)}, u32[]{:S(2)}) async-start(bf16[8,64,1024]{2,1,0:T(8,128)(2,1)} %bitcast.25), calls=%async_computation.3 | async-start | bytes 2097152 | tf_op jit(solution)/shard_map/all_to_all | solution.py:109
  116.2 58.6 %copy-start.31 = (f32[512]{0:T(512)}, f32[512]{0:T(512)S(1)}, u32[]{:S(2)}) copy-start(f32[512]{0:T(512)S(1)} %get-tuple-element.49) | copy-start | bytes 6148
  116.6 61.7 %copy-start.30 = (f32[512]{0:T(512)}, f32[512]{0:T(512)S(1)}, u32[]{:S(2)}) copy-start(f32[512]{0:T(512)S(1)} %get-tuple-element.53) | copy-start | bytes 6148
  117.1 61.1 %copy-start.41 = (f32[512]{0:T(512)}, f32[512]{0:T(512)S(1)}, u32[]{:S(2)}) copy-start(f32[512]{0:T(512)S(1)} %fusion.76) | copy-start | bytes 6148
  117.3 62.3 %copy-start.40 = (f32[512]{0:T(512)}, f32[512]{0:T(512)S(1)}, u32[]{:S(2)}) copy-start(f32[512]{0:T(512)S(1)} %fusion.78) | copy-start | bytes 6148
  118.1 63.6 %copy-start.39 = (f32[512]{0:T(512)}, f32[512]{0:T(512)S(1)}, u32[]{:S(2)}) copy-start(f32[512]{0:T(512)S(1)} %fusion.80) | copy-start | bytes 6148
  118.7 65.2 %copy-start.38 = (f32[512]{0:T(512)}, f32[512]{0:T(512)S(1)}, u32[]{:S(2)}) copy-start(f32[512]{0:T(512)S(1)} %fusion.82) | copy-start | bytes 6148
  119.1 67.0 %copy-start.2 = (f32[512,512]{0,1:T(8,128)}, f32[512,512]{0,1:T(8,128)S(1)}, u32[]{:S(2)}) copy-start(f32[512,512]{0,1:T(8,128)S(1)} %get-tuple-element.66) | copy-start | bytes 3145732
  119.3 66.8 %copy-start.37 = (f32[512]{0:T(512)}, f32[512]{0:T(512)S(1)}, u32[]{:S(2)}) copy-start(f32[512]{0:T(512)S(1)} %fusion.84) | copy-start | bytes 6148
  120.7 66.9 %copy-start = (f32[512,512]{0,1:T(8,128)}, f32[512,512]{0,1:T(8,128)S(1)}, u32[]{:S(2)}) copy-start(f32[512,512]{0,1:T(8,128)S(1)} %get-tuple-element.70) | copy-start | bytes 3145732
  121.0 66.7 %copy-start.36 = (f32[512]{0:T(512)}, f32[512]{0:T(512)S(1)}, u32[]{:S(2)}) copy-start(f32[512]{0:T(512)S(1)} %fusion.86) | copy-start | bytes 6148
  192.6 36.0 %all-to-all-start.4 = ((bf16[8,64,1024]{2,1,0:T(8,128)(2,1)}), bf16[8,64,1024]{2,1,0:T(8,128)(2,1)S(1)}, u32[]{:S(2)}, u32[]{:S(2)}) async-start(bf16[8,64,1024]{2,1,0:T(8,128)(2,1)} %bitcast.27), calls=%async_computation.4 | async-start | bytes 2097152 | tf_op jit(solution)/shard_map/all_to_all | solution.py:135
  228.5 28.3 %all-to-all-start.5 = ((bf16[8,64,1024]{2,1,0:T(8,128)(2,1)}), bf16[8,64,1024]{2,1,0:T(8,128)(2,1)S(1)}, u32[]{:S(2)}, u32[]{:S(2)}) async-start(bf16[8,64,1024]{2,1,0:T(8,128)(2,1)} %bitcast.132), calls=%async_computation.6 | async-start | bytes 2097152 | tf_op jit(solution)/shard_map/all_to_all | solution.py:149
  234.5 164.3 %reduce-scatter.2.cloned.1.call-start = ((), (), s32[]{:S(2)}) async-start(), calls=%async_computation.11 | async-start | bytes 2621440 | tf_op jit(solution)/shard_map/reduce_scatter | solution.py:139
  307.7 29.4 %all-to-all-start.7 = ((bf16[8,64,1024]{2,1,0:T(8,128)(2,1)}), bf16[8,64,1024]{2,1,0:T(8,128)(2,1)S(1)}, u32[]{:S(2)}, u32[]{:S(2)}) async-start(bf16[8,64,1024]{2,1,0:T(8,128)(2,1)} %bitcast.131), calls=%async_computation.8 | async-start | bytes 2097152 | tf_op jit(solution)/shard_map/all_to_all | solution.py:157
  337.1 29.6 %all-to-all-start.6 = ((bf16[8,64,1024]{2,1,0:T(8,128)(2,1)}), bf16[8,64,1024]{2,1,0:T(8,128)(2,1)S(1)}, u32[]{:S(2)}, u32[]{:S(2)}) async-start(bf16[8,64,1024]{2,1,0:T(8,128)(2,1)} %bitcast.130), calls=%async_computation.7 | async-start | bytes 2097152 | tf_op jit(solution)/shard_map/all_to_all | solution.py:156
  366.7 29.6 %all-to-all-start.8 = ((bf16[8,64,1024]{2,1,0:T(8,128)(2,1)}), bf16[8,64,1024]{2,1,0:T(8,128)(2,1)S(1)}, u32[]{:S(2)}, u32[]{:S(2)}) async-start(bf16[8,64,1024]{2,1,0:T(8,128)(2,1)} %bitcast.133), calls=%async_computation.9 | async-start | bytes 2097152 | tf_op jit(solution)/shard_map/all_to_all | solution.py:158
  (37 other events, 551.9 us)
Sparse Core Ops, SparseCore 0:
  9.6 23.5 all-gather.4
  35.2 184.2 all-gather.2
  244.0 32.1 reduce-scatter.1
where the time goes:
time: 412 us; the launch traced here: 405 us
  waiting for transfers between devices  166 us (40%)
  matrix products  95.2 us (23%)
  starting transfers between devices  57.3 us (14%)
  local copies, waits for them, and re-layouts  43.7 us (11%)
  other arithmetic  28.9 us (7%)
  between operations  14.3 us (3%)
    all_to_all x1, waiting for transfers between devices, on_device(): lax.all_to_all(to_slots(value_rows), 'seq', split_axis=0, concat_axis=0,...  47.3 us
    all_to_all x1, waiting for transfers between devices, on_device(): lax.all_to_all(to_slots(queries), 'seq', split_axis=0, concat_axis=0, til...  36.3 us
    all_to_all x1, waiting for transfers between devices, on_device(): lax.all_to_all(grad_v, 'seq', split_axis=0, concat_axis=0, tiled=True)  20.5 us
    all_gather x1, waiting for transfers between devices, on_device(): full_weight = lax.all_gather(out_weight, 'seq', axis=1, tiled=True)  19.6 us
    all_to_all x1, waiting for transfers between devices, on_device(): lax.all_to_all(to_slots(key_rows), 'seq', split_axis=0, concat_axis=0, ti...  17.4 us
    dot_general x8, matrix products, attend_back(): jnp.einsum('qd,kd->qk', grad_head, value_head, preferred_element_type=jnp...  17.2 us
    dot_general x8, matrix products, attend_back(): jnp.einsum('qk,qd->kd', probs_low, grad_head, preferred_element_type=jnp....  16 us
    dot_general x8, matrix products, attend_back(): jnp.dot(dscores, key_head, preferred_element_type=jnp.float32) * score_scale  15.7 us
  transfers between devices with their start and end apart: 12, of which 8 were waited for; matrix products, arithmetic and copies ran while one was open for 41% of the time, Pallas kernels for 0%

commit v1 on v0

--- a/solution.py
+++ b/solution.py
@@ -1,8 +1,11 @@
+import functools
 import math
 
 import jax
 import jax.numpy as jnp
 from jax import lax
+from jax.experimental import pallas as pl
+from jax.experimental.pallas import tpu as pltpu
 from jax.sharding import PartitionSpec as P
 
 HD = 128
@@ -76,7 +79,7 @@
     )
 
 
-def on_device(queries, key_rows, value_rows, out_weight, grad_output, cluster_ids, block_pattern):
+def by_clusters(queries, key_rows, value_rows, out_weight, grad_output, cluster_ids, block_pattern):
     tokens = queries.shape[0]
     width = queries.shape[1]
     head_count = width // HD
@@ -160,6 +163,210 @@
     return (layer_out, from_slots(back_q), from_slots(back_k), from_slots(back_v))
 
 
+ID_ROWS = 16
+
+
+def one_hot(hit):
+    return jnp.where(hit, 1.0, 0.0).astype(jnp.bfloat16)
+
+
+def dot_rows(left, right):
+    return lax.dot_general(
+        left, right, (((1,), (0,)), ((), ())), preferred_element_type=jnp.float32
+    )
+
+
+def dot_last(left, right):
+    return lax.dot_general(
+        left, right, (((1,), (1,)), ((), ())), preferred_element_type=jnp.float32
+    )
+
+
+def dot_first(left, right):
+    return lax.dot_general(
+        left, right, (((0,), (0,)), ((), ())), preferred_element_type=jnp.float32
+    )
+
+
+def cluster_places(arrived_ref, rows, parts, place_ref, place_cols_ref):
+    before = lax.broadcasted_iota(jnp.int32, (rows, rows), 0)
+    after = lax.broadcasted_iota(jnp.int32, (rows, rows), 1)
+    strict = one_hot(before < after)
+    names = lax.broadcasted_iota(jnp.int32, (parts, rows), 0).astype(jnp.float32)
+    seen = jnp.zeros((parts, 1), jnp.float32)
+    lines = []
+    for part in range(parts):
+        ids = jnp.concatenate(
+            [
+                arrived_ref[part, 3 * rows + i : 3 * rows + i + 1, :].astype(jnp.float32)
+                for i in range(rows // HD)
+            ],
+            axis=1,
+        )
+        hit = names == ids
+        mark = jnp.where(hit, 1.0, 0.0)
+        rank = dot_rows(mark.astype(jnp.bfloat16), strict) + seen
+        lines.append(jnp.sum(mark * (rank + names * rows), axis=0, keepdims=True))
+        seen = seen + jnp.sum(mark, axis=1, keepdims=True)
+    places = jnp.concatenate(lines, axis=0)
+    place_ref[...] = places
+    padded = jnp.concatenate([places, jnp.zeros((HD - parts, rows), jnp.float32)], axis=0)
+    place_cols_ref[...] = padded.T
+
+
+def to_cluster(place_ref, rows, parts, cluster, read_part):
+    want = lax.broadcasted_iota(jnp.int32, (rows, rows), 0).astype(jnp.float32) + (
+        cluster * rows
+    ).astype(jnp.float32)
+    total = None
+    for part in range(parts):
+        pick = one_hot(want == place_ref[part : part + 1, :])
+        term = dot_rows(pick, read_part(part))
+        total = term if total is None else total + term
+    return total.astype(jnp.bfloat16)
+
+
+def from_clusters(place_cols_ref, rows, parts, part, ordered):
+    lanes = lax.broadcasted_iota(jnp.int32, (rows, parts * rows), 1).astype(jnp.float32)
+    pick = one_hot(place_cols_ref[:, part : part + 1] == lanes)
+    return dot_rows(pick, ordered).astype(jnp.bfloat16)
+
+
+def cluster_probs(pattern_ref, cluster, query, key, rows, score_scale):
+    scores = dot_last(query, key) * score_scale
+    row_at = lax.broadcasted_iota(jnp.int32, (rows, rows), 0)
+    col_at = lax.broadcasted_iota(jnp.int32, (rows, rows), 1)
+    reads = pattern_ref[cluster * 4 + 2]
+    ok = (col_at <= row_at) & ((row_at // BLK == col_at // BLK) | (reads == 1))
+    scores = jnp.where(ok, scores, -jnp.inf)
+    shifted = jnp.exp(scores - jnp.max(scores, axis=1, keepdims=True))
+    return shifted / jnp.sum(shifted, axis=1, keepdims=True)
+
+
+def forward_kernel(
+    rows, parts, pattern_ref, arrived_ref, mixed_ref, sorted_ref, place_ref, place_cols_ref, held
+):
+    score_scale = 1.0 / math.sqrt(HD)
+    cluster_places(arrived_ref, rows, parts, place_ref, place_cols_ref)
+
+    def step(cluster, _):
+        def read_part(part):
+            return jnp.concatenate(
+                [arrived_ref[part, i * rows : (i + 1) * rows, :] for i in range(3)], axis=1
+            )
+
+        picked = to_cluster(place_ref, rows, parts, cluster, read_part)
+        sorted_ref[cluster] = picked
+        query, key, value = (picked[:, i * HD : (i + 1) * HD] for i in range(3))
+        probs = cluster_probs(pattern_ref, cluster, query, key, rows, score_scale)
+        at = pl.multiple_of(cluster * rows, rows)
+        held[pl.ds(at, rows), :] = dot_rows(probs.astype(jnp.bfloat16), value).astype(jnp.bfloat16)
+        return 0
+
+    lax.fori_loop(0, parts, step, 0, unroll=2)
+    for part in range(parts):
+        mixed_ref[part] = from_clusters(place_cols_ref, rows, parts, part, held[...])
+
+
+def backward_kernel(
+    rows, parts, pattern_ref, sorted_ref, place_ref, place_cols_ref, grad_ref, out_ref, held
+):
+    score_scale = 1.0 / math.sqrt(HD)
+
+    def step(cluster, _):
+        grad = to_cluster(place_ref, rows, parts, cluster, lambda part: grad_ref[part])
+        picked = sorted_ref[cluster]
+        query, key, value = (picked[:, i * HD : (i + 1) * HD] for i in range(3))
+        probs = cluster_probs(pattern_ref, cluster, query, key, rows, score_scale)
+        low = probs.astype(jnp.bfloat16)
+        mixed = dot_rows(low, value).astype(jnp.bfloat16).astype(jnp.float32)
+        delta = jnp.sum(grad.astype(jnp.float32) * mixed, axis=1, keepdims=True)
+        dscores = (probs * (dot_last(grad, value) - delta)).astype(jnp.bfloat16)
+        at = pl.multiple_of(cluster * rows, rows)
+        here = pl.ds(at, rows)
+        held[here, 0:HD] = (dot_rows(dscores, key) * score_scale).astype(jnp.bfloat16)
+        held[here, HD : 2 * HD] = (dot_first(dscores, query) * score_scale).astype(jnp.bfloat16)
+        held[here, 2 * HD : 3 * HD] = dot_first(low, grad).astype(jnp.bfloat16)
+        return 0
+
+    lax.fori_loop(0, parts, step, 0, unroll=2)
+    for part in range(parts):
+        back = from_clusters(place_cols_ref, rows, parts, part, held[...])
+        for i in range(3):
+            out_ref[part, i * rows : (i + 1) * rows, :] = back[:, i * HD : (i + 1) * HD]
+
+
+VMEM_SPEC = pl.BlockSpec(memory_space=pltpu.VMEM)
+SMEM_SPEC = pl.BlockSpec(memory_space=pltpu.SMEM)
+PARAMS = pltpu.CompilerParams(vmem_limit_bytes=48 * 1024 * 1024)
+
+
+def by_heads(queries, key_rows, value_rows, out_weight, grad_output, cluster_ids, block_pattern):
+    rows, width = queries.shape
+    parts = lax.axis_size("seq")
+    pattern = block_pattern.reshape(-1)
+
+    def heads_first(row_data):
+        return row_data.reshape(rows, parts, HD).transpose(1, 0, 2)
+
+    def heads_last(row_data):
+        return row_data.transpose(1, 0, 2).reshape(rows, width)
+
+    def swap(buffer):
+        return lax.all_to_all(buffer, "seq", split_axis=0, concat_axis=0, tiled=True)
+
+    id_rows = jnp.zeros((ID_ROWS, HD), jnp.bfloat16)
+    id_rows = id_rows.at[: rows // HD].set(cluster_ids.reshape(-1, HD).astype(jnp.bfloat16))
+    id_rows = jnp.broadcast_to(id_rows[None], (parts, ID_ROWS, HD))
+    packed = jnp.concatenate(
+        [heads_first(queries), heads_first(key_rows), heads_first(value_rows), id_rows], axis=1
+    )
+    full_weight = lax.all_gather(out_weight, "seq", axis=1, tiled=True)
+    full_grad = lax.all_gather(grad_output, "head", axis=1, tiled=True)
+    arrived = swap(packed)
+    mixed, ordered, places, place_cols = pl.pallas_call(
+        functools.partial(forward_kernel, rows, parts),
+        out_shape=(
+            jax.ShapeDtypeStruct((parts, rows, HD), jnp.bfloat16),
+            jax.ShapeDtypeStruct((parts, rows, 3 * HD), jnp.bfloat16),
+            jax.ShapeDtypeStruct((parts, rows), jnp.float32),
+            jax.ShapeDtypeStruct((rows, HD), jnp.float32),
+        ),
+        in_specs=[SMEM_SPEC, VMEM_SPEC],
+        out_specs=(VMEM_SPEC,) * 4,
+        scratch_shapes=[pltpu.VMEM((parts * rows, HD), jnp.bfloat16)],
+        compiler_params=PARAMS,
+        name="attention_forward",
+    )(pattern, arrived)
+    attn_local = heads_last(swap(mixed))
+    grad_attention = jnp.einsum(
+        "td,wd->tw", full_grad, full_weight, preferred_element_type=jnp.float32
+    ).astype(jnp.bfloat16)
+    grad_in = swap(heads_first(grad_attention))
+    grads = pl.pallas_call(
+        functools.partial(backward_kernel, rows, parts),
+        out_shape=jax.ShapeDtypeStruct((parts, 3 * rows, HD), jnp.bfloat16),
+        in_specs=[SMEM_SPEC] + [VMEM_SPEC] * 4,
+        out_specs=VMEM_SPEC,
+        scratch_shapes=[pltpu.VMEM((parts * rows, 3 * HD), jnp.bfloat16)],
+        compiler_params=PARAMS,
+        name="attention_backward",
+    )(pattern, ordered, places, place_cols, grad_in)
+    partial_value = jnp.dot(attn_local, full_weight, preferred_element_type=jnp.float32)
+    layer_out = lax.psum_scatter(
+        partial_value.astype(jnp.bfloat16), "head", scatter_dimension=1, tiled=True
+    )
+    back = swap(grads)
+    return (layer_out,) + tuple(heads_last(back[:, i * rows : (i + 1) * rows]) for i in range(3))
+
+
+def on_device(queries, *others):
+    heads = queries.shape[1] // HD
+    if heads == lax.axis_size("seq") and others[-1].shape[1] == 2:
+        return by_heads(queries, *others)
+    return by_clusters(queries, *others)
+
+
 def solution(mesh):
     in_specs = (
         P("seq", "head"),

time: 412 us -> 295 us (0.72)
  blocking collectives: 0 us -> 83 us
  matrix products: 95.2 us -> 13.5 us
  starting transfers between devices: 57.3 us -> 6.21 us
  local copies, waits for them, and re-layouts: 43.7 us -> 7.19 us
  other arithmetic: 28.9 us -> 1.26 us
  waiting for transfers between devices: 166 us -> 141 us
  Pallas kernels: 0 us -> 24.8 us
    all_to_all x0 -> x3, blocking collectives: none -> 83 us  [swap(): lax.all_to_all(buffer, 'seq', split_axis=0, concat_axis=0, tiled=True)]
    dot_general x51 -> x2, matrix products: 95.2 us -> 13.5 us  [the longest x1 7.09 us: by_heads(): jnp.dot(attn_local, full_weight, preferred_element_type=jnp.float32)]
    all_to_all x9 -> x1, waiting for transfers between devices: 145 us -> 68 us  [swap(): lax.all_to_all(buffer, 'seq', split_axis=0, concat_axis=0, tiled=True)]
    all_gather x2, waiting for transfers between devices: 19.6 us -> 72 us  [the longest x1 54 us: by_heads(): full_weight = lax.all_gather(out_weight, 'seq', axis=1, tiled=True)]
    all_to_all x9 -> x1, starting transfers between devices: 57.2 us -> 6.13 us  [swap(): lax.all_to_all(buffer, 'seq', split_axis=0, concat_axis=0, tiled=True)]
    pallas_call x0 -> x2, Pallas kernels: none -> 24.8 us  [the longest x1 13.6 us: by_heads(): pl.pallas_call(functools.partial(backward_kernel, rows, parts), out_shape...]
    scatter x4 -> x1, local copies, waits for them, and re-layouts: 12.1 us -> 0.01 us  [by_heads(): id_rows.at[:rows // HD]]
    concatenate x4 -> x0, local copies, waits for them, and re-layouts: 9.14 us -> none  [the longest x1 2.29 us: attend(): return jnp.concatenate(results, axis=1)]
  transfers between devices with their start and end apart: 12 -> 4, of which waited for: 8 -> 3; matrix products, arithmetic and copies ran while one was open for 41% -> 8% of each run, Pallas kernels for 0% -> 9%
where the time goes in v1:
time: 295 us; the launch traced here: 291 us
  waiting for transfers between devices  141 us (48%)
  blocking collectives  83 us (28%)
  Pallas kernels  24.8 us (8%)
  between operations  13.9 us (5%)
  matrix products  13.5 us (5%)
  local copies, waits for them, and re-layouts  7.19 us (2%)
  starting transfers between devices  6.21 us (2%)
    all_to_all x3, blocking collectives, swap(): lax.all_to_all(buffer, 'seq', split_axis=0, concat_axis=0, tiled=True)  83 us
    all_to_all x1, waiting for transfers between devices, swap(): lax.all_to_all(buffer, 'seq', split_axis=0, concat_axis=0, tiled=True)  68 us
    all_gather x1, waiting for transfers between devices, by_heads(): full_weight = lax.all_gather(out_weight, 'seq', axis=1, tiled=True)  54 us
    all_gather x1, waiting for transfers between devices, by_heads(): full_grad = lax.all_gather(grad_output, 'head', axis=1, tiled=True)  18 us
    pallas_call x1, Pallas kernels, by_heads(): pl.pallas_call(functools.partial(backward_kernel, rows, parts), out_shape...  13.6 us
    pallas_call x1, Pallas kernels, by_heads(): pl.pallas_call(functools.partial(forward_kernel, rows, parts), out_shape=...  11.1 us
    dot_general x1, matrix products, by_heads(): jnp.dot(attn_local, full_weight, preferred_element_type=jnp.float32)  7.09 us
    dot_general x1, matrix products, by_heads(): jnp.einsum('td,wd->tw', full_grad, full_weight, preferred_element_type=jn...  6.38 us
  transfers between devices with their start and end apart: 4, of which 3 were waited for; matrix products, arithmetic and copies ran while one was open for 8% of the time, Pallas kernels for 9%

profile of v1, /device:TPU:28, one launch (start us, length us, event | category | flops | bytes accessed | tf_op | source)
XLA Modules:
  0.0 291.3 jit_solution(3835059795958574567)
XLA Ops:
  7.2 0.7 all-gather.3.cloned.1.call-update
  7.9 1.3 copy.13
  9.2 0.3 copy.14
  9.7 0.3 copy.16
  10.2 0.3 copy.18
  10.6 1.3 pad_maximum_fusion
  11.8 6.1 %all-to-all-start = ((bf16[8,784,128]{2,1,0:T(8,128)(2,1)}), bf16[8,784,128]{2,1,0:T(8,128)(2,1)S(1)}, u32[]{:S(2)}, u32[]{:S(2)}) async-start(bf16[8,784,128]{2,1,0:T(8,128)(2,1)} %pad_maximum_fusion), calls=%async_computation | async-start | bytes 3211264 | tf_op jit(solution)/shard_map/all_to_all | solution.py:316
  17.9 0.7 all-gather.5.cloned.1.call-update
  18.9 68.0 %all-to-all-done.arrived_ref = bf16[8,784,128]{2,1,0:T(8,128)(2,1)S(1)} async-done(((bf16[8,784,128]{2,1,0:T(8,128)(2,1)}), bf16[8,784,128]{2,1,0:T(8,128)(2,1)S(1)}, u32[]{:S(2)}, u32[]{:S(2)}) %all-to-all-start) | async-done | bytes 1605664 | tf_op jit(solution)/shard_map/all_to_all | solution.py:316
  86.9 11.1 %attention_forward.1 = (bf16[8,256,128]{2,1,0:T(8,128)(2,1)S(1)}, bf16[8,256,384]{2,1,0:T(8,128)(2,1)S(1)}, f32[8,256]{1,0:T(8,128)S(1)}, f32[256,128]{1,0:T(8,128)S(1)}) custom-call(s32[32]{0:T(128)S(1)} %reshape.70.pattern_ref, bf16[8,784,128]{2,1,0:T(8,128)(2,1)S(1)} %all-to-all-done.arrived_ref), custom_call_target="tpu_custom_call" | custom-call | tf_op jit(solution)/shard_map/attention_forward/pallas_call | solution.py:327
  98.1 24.4 %all_to_all.20 = bf16[8,256,128]{2,1,0:T(8,128)(2,1)S(1)} all-to-all(bf16[8,256,128]{2,1,0:T(8,128)(2,1)S(1)} %get-tuple-element.20), channel_id=1, replica_groups=mesh['seq'=8,'head'=4] {'seq'}, dimensions={0} | all-to-all | bytes 1048576 | tf_op jit(solution)/shard_map/all_to_all | solution.py:316
  122.4 0.2 copy.19
  122.7 54.0 %all-gather.3.cloned.1.call-done = bf16[1024,4096]{1,0:T(8,128)(2,1)} async-done(((bf16[1024,512]{1,0:T(8,128)(2,1)}), bf16[1024,4096]{1,0:T(8,128)(2,1)}) %all-gather.3.cloned.1.call-update) | async-done | bytes 8388624 | tf_op jit(solution)/shard_map/all_gather | solution.py:324
  176.7 7.1 %convolution_convert_fusion = bf16[256,4096]{1,0:T(8,128)(2,1)} fusion(bf16[256,1024]{0,1:T(8,128)(2,1)S(1)} %bitcast.25, bf16[1024,4096]{1,0:T(8,128)(2,1)} %all-gather.3.cloned.1.call-done), kind=kOutput, calls=%fused_computation | convolution fusion | flops 2148532224 | bytes 11010048 | tf_op jit(solution)/shard_map/dot_general | solution.py:355
  183.8 18.0 %all-gather.5.cloned.1.call-done = bf16[256,4096]{1,0:T(8,128)(2,1)} async-done(((bf16[256,1024]{1,0:T(8,128)(2,1)}), bf16[256,4096]{1,0:T(8,128)(2,1)}) %all-gather.5.cloned.1.call-update) | async-done | bytes 2097168 | tf_op jit(solution)/shard_map/all_gather | solution.py:325
  201.8 6.4 %convolution_convert_fusion.1 = bf16[256,1024]{1,0:T(8,128)(2,1)S(1)} fusion(bf16[256,4096]{1,0:T(8,128)(2,1)} %all-gather.5.cloned.1.call-done, bf16[1024,4096]{1,0:T(8,128)(2,1)} %all-gather.3.cloned.1.call-done), kind=kOutput, calls=%fused_computation.2 | convolution fusion | flops 2147745792 | bytes 11010048 | tf_op jit(solution)/shard_map/td,wd->tw/dot_general | solution.py:342
  208.4 0.3 copy.21
  208.6 18.3 %all_to_all.21.grad_ref = bf16[8,256,128]{2,1,0:T(8,128)(2,1)S(1)} all-to-all(bf16[8,256,128]{2,1,0:T(8,128)(2,1)S(1)} %bitcast.31), channel_id=1, replica_groups=mesh['seq'=8,'head'=4] {'seq'}, dimensions={0} | all-to-all | bytes 1048576 | tf_op jit(solution)/shard_map/all_to_all | solution.py:316
  227.0 13.6 %attention_backward.1 = bf16[8,768,128]{2,1,0:T(8,128)(2,1)S(1)} custom-call(s32[32]{0:T(128)S(1)} %reshape.70.pattern_ref, bf16[8,256,384]{2,1,0:T(8,128)(2,1)S(1)} %get-tuple-element.21.sorted_ref, f32[8,256]{1,0:T(8,128)S(1)} %get-tuple-element.22.place_ref, f32[256,128]{1,0:T(8,128)S(1)} %get-tuple-element.23.place_cols_ref, ...), custom_call_target="tpu_custom_call" | custom-call | tf_op jit(solution)/shard_map/attention_backward/pallas_call | solution.py:346
  240.6 40.4 %all_to_all.22 = bf16[8,768,128]{2,1,0:T(8,128)(2,1)S(1)} all-to-all(bf16[8,768,128]{2,1,0:T(8,128)(2,1)S(1)} %attention_backward.1), channel_id=1, replica_groups=mesh['seq'=8,'head'=4] {'seq'}, dimensions={0} | all-to-all | bytes 3145728 | tf_op jit(solution)/shard_map/all_to_all | solution.py:316
  281.1 0.2 copy.24
  281.3 1.0 copy.27
  282.5 1.0 copy.26
  283.7 1.0 copy.25
  (24 shorter events, 1.5 us)
Async XLA Ops:
  7.2 2.3 copy-start
  7.2 169.5 %all-gather.3.cloned.1.call-start = ((), (), s32[]{:S(2)}) async-start(), calls=%async_computation.5 | async-start | bytes 9437184 | tf_op jit(solution)/shard_map/all_gather | solution.py:324
  7.9 2.1 copy-start.1
  9.5 1.0 copy-start.3
  11.8 6.9 %copy-start.2 = (s32[8,2,2]{0,2,1:T(2,128)S(1)}, s32[8,2,2]{0,2,1:T(2,128)}, u32[]{:S(2)}) copy-start(s32[8,2,2]{0,2,1:T(2,128)} %param.15) | copy-start | bytes 388
  11.8 75.1 %all-to-all-start = ((bf16[8,784,128]{2,1,0:T(8,128)(2,1)}), bf16[8,784,128]{2,1,0:T(8,128)(2,1)S(1)}, u32[]{:S(2)}, u32[]{:S(2)}) async-start(bf16[8,784,128]{2,1,0:T(8,128)(2,1)} %pad_maximum_fusion), calls=%async_computation | async-start | bytes 3211264 | tf_op jit(solution)/shard_map/all_to_all | solution.py:316
  17.9 183.8 %all-gather.5.cloned.1.call-start = ((), (), s32[]{:S(2)}) async-start(), calls=%async_computation.7 | async-start | bytes 2621440 | tf_op jit(solution)/shard_map/all_gather | solution.py:325
  18.7 266.1 %reduce-scatter.2.cloned.1.call-start = ((), (), s32[]{:S(2)}) async-start(), calls=%async_computation.6 | async-start | bytes 2621440 | tf_op jit(solution)/shard_map/reduce_scatter | solution.py:356
Sparse Core Ops, SparseCore 0:
  10.1 166.5 all-gather.2
  178.2 23.4 all-gather.4
  204.9 31.4 reduce-scatter.1

commit v2 on v0

--- a/solution.py
+++ b/solution.py
@@ -1,8 +1,11 @@
+import functools
 import math
 
 import jax
 import jax.numpy as jnp
 from jax import lax
+from jax.experimental import pallas as pl
+from jax.experimental.pallas import tpu as pltpu
 from jax.sharding import PartitionSpec as P
 
 HD = 128
@@ -76,7 +79,7 @@
     )
 
 
-def on_device(queries, key_rows, value_rows, out_weight, grad_output, cluster_ids, block_pattern):
+def by_clusters(queries, key_rows, value_rows, out_weight, grad_output, cluster_ids, block_pattern):
     tokens = queries.shape[0]
     width = queries.shape[1]
     head_count = width // HD
@@ -160,6 +163,384 @@
     return (layer_out, from_slots(back_q), from_slots(back_k), from_slots(back_v))
 
 
+ID_ROWS = 16
+MESH = pl.DeviceIdType.MESH
+
+
+def one_hot(hit):
+    return jnp.where(hit, 1.0, 0.0).astype(jnp.bfloat16)
+
+
+def dot_rows(left, right):
+    return lax.dot_general(
+        left, right, (((1,), (0,)), ((), ())), preferred_element_type=jnp.float32
+    )
+
+
+def dot_last(left, right):
+    return lax.dot_general(
+        left, right, (((1,), (1,)), ((), ())), preferred_element_type=jnp.float32
+    )
+
+
+def dot_first(left, right):
+    return lax.dot_general(
+        left, right, (((0,), (0,)), ((), ())), preferred_element_type=jnp.float32
+    )
+
+
+def cluster_places(ids_ref, rows, parts, place_ref, place_cols_ref):
+    before = lax.broadcasted_iota(jnp.int32, (rows, rows), 0)
+    after = lax.broadcasted_iota(jnp.int32, (rows, rows), 1)
+    strict = one_hot(before < after)
+    names = lax.broadcasted_iota(jnp.int32, (parts, rows), 0).astype(jnp.float32)
+    seen = jnp.zeros((parts, 1), jnp.float32)
+    lines = []
+    for part in range(parts):
+        ids = jnp.concatenate(
+            [
+                ids_ref[part, i : i + 1, :].astype(jnp.float32)
+                for i in range(rows // HD)
+            ],
+            axis=1,
+        )
+        hit = names == ids
+        mark = jnp.where(hit, 1.0, 0.0)
+        rank = dot_rows(mark.astype(jnp.bfloat16), strict) + seen
+        lines.append(jnp.sum(mark * (rank + names * rows), axis=0, keepdims=True))
+        seen = seen + jnp.sum(mark, axis=1, keepdims=True)
+    places = jnp.concatenate(lines, axis=0)
+    place_ref[...] = places
+    padded = jnp.concatenate([places, jnp.zeros((HD - parts, rows), jnp.float32)], axis=0)
+    place_cols_ref[...] = padded.T
+
+
+def to_cluster(place_ref, rows, parts, cluster, read_part):
+    want = lax.broadcasted_iota(jnp.int32, (rows, rows), 0).astype(jnp.float32) + (
+        cluster * rows
+    ).astype(jnp.float32)
+    total = None
+    for part in range(parts):
+        pick = one_hot(want == place_ref[part : part + 1, :])
+        term = dot_rows(pick, read_part(part))
+        total = term if total is None else total + term
+    return total.astype(jnp.bfloat16)
+
+
+def from_clusters(place_cols_ref, rows, parts, part, ordered):
+    lanes = lax.broadcasted_iota(jnp.int32, (rows, parts * rows), 1).astype(jnp.float32)
+    pick = one_hot(place_cols_ref[:, part : part + 1] == lanes)
+    return dot_rows(pick, ordered).astype(jnp.bfloat16)
+
+
+def cluster_probs(pattern_ref, cluster, query, key, rows, score_scale):
+    scores = dot_last(query, key) * score_scale
+    row_at = lax.broadcasted_iota(jnp.int32, (rows, rows), 0)
+    col_at = lax.broadcasted_iota(jnp.int32, (rows, rows), 1)
+    reads = pattern_ref[cluster * 4 + 2]
+    ok = (col_at <= row_at) & ((row_at // BLK == col_at // BLK) | (reads == 1))
+    scores = jnp.where(ok, scores, -jnp.inf)
+    shifted = jnp.exp(scores - jnp.max(scores, axis=1, keepdims=True))
+    return shifted / jnp.sum(shifted, axis=1, keepdims=True)
+
+
+def layer_kernel(
+    rows, parts, groups, pattern_ref, ids_ref, q_ref, k_ref, v_ref, w_ref, g_ref,
+    out_ref, gq_ref, gk_ref, gv_ref,
+    q_in, k_in, v_in, ids_in, weight, cotangent, places, place_cols, ordered, probs_at, held,
+    mixed_send, attn, grad_sum, grad_send, grad_in, dscores_at, held_qk, held_v, back_q, back_k, back_v,
+    partial, shares,
+    tok_send, tok_recv, ring_send, ring_recv, head_send, head_recv, own_sem,
+):
+    score_scale = 1.0 / math.sqrt(HD)
+    me = lax.axis_index("seq")
+    group = lax.axis_index("head")
+    half = w_ref.shape[0] // 2
+    cols = w_ref.shape[1]
+
+    def other(j):
+        return lax.rem(me + j, parts)
+
+    def other_group(j):
+        return lax.rem(group + j, groups)
+
+    def head_at(index):
+        return pl.ds(pl.multiple_of(index * HD, HD), HD)
+
+    def along_seq(kind, j, source, target):
+        return pltpu.make_async_remote_copy(
+            src_ref=source, dst_ref=target, send_sem=tok_send.at[kind, j],
+            recv_sem=tok_recv.at[kind, j], device_id={"seq": other(j)}, device_id_type=MESH,
+        )
+
+    def along_head(kind, j, source, target):
+        return pltpu.make_async_remote_copy(
+            src_ref=source, dst_ref=target, send_sem=head_send.at[kind, j],
+            recv_sem=head_recv.at[kind, j], device_id={"head": other_group(j)}, device_id_type=MESH,
+        )
+
+    line = parts // 2
+    row, side = me // 2, lax.rem(me, 2)
+    place = row + side * (parts - 1 - 2 * row)
+
+    def at_place(p):
+        p = lax.rem(p + 2 * parts, parts)
+        far = p // line
+        return 2 * (p + far * (parts - 1 - 2 * p)) + far
+
+    def ring(way, step):
+        sign = 1 - 2 * way
+        block = weight.at[at_place(place - sign * step), pl.ds(way * half, half)]
+        return pltpu.make_async_remote_copy(
+            src_ref=block, dst_ref=block, send_sem=ring_send.at[way, step],
+            recv_sem=ring_recv.at[way, step], device_id={"seq": at_place(place + sign)},
+            device_id_type=MESH,
+        )
+
+    own_weight = pltpu.make_async_copy(w_ref, weight.at[me], own_sem.at[0])
+    own_weight.start()
+    for i in range(2):
+        cotangent[2 * group + i] = g_ref[:, i * cols : (i + 1) * cols]
+
+    barrier = pltpu.get_barrier_semaphore()
+    for j in range(1, parts):
+        pl.semaphore_signal(barrier, inc=1, device_id={"seq": other(j)}, device_id_type=MESH)
+    for j in range(1, groups):
+        pl.semaphore_signal(barrier, inc=1, device_id={"head": other_group(j)}, device_id_type=MESH)
+    pl.semaphore_wait(barrier, parts + groups - 2)
+
+    own_weight.wait()
+    for way in range(2):
+        ring(way, 0).start()
+
+    def head_copies(j):
+        block = cotangent.at[pl.ds(2 * group, 2)]
+        return along_head(0, j, block, block)
+
+    for j in range(1, groups):
+        head_copies(j).start()
+
+    def token_copies(j):
+        dest = head_at(other(j))
+        return (
+            along_seq(0, j, q_ref.at[:, dest], q_in.at[me]),
+            along_seq(1, j, k_ref.at[:, dest], k_in.at[me]),
+            along_seq(2, j, v_ref.at[:, dest], v_in.at[me]),
+            along_seq(3, j, ids_ref, ids_in.at[me]),
+        )
+
+    for j in range(1, parts):
+        for copy in token_copies(j):
+            copy.start()
+    q_in[me] = q_ref[:, head_at(me)]
+    k_in[me] = k_ref[:, head_at(me)]
+    v_in[me] = v_ref[:, head_at(me)]
+    ids_in[me] = ids_ref[...]
+
+    grad_sum[...] = jnp.zeros_like(grad_sum)
+
+    for j in range(1, groups):
+        head_copies(j).wait()
+
+    def accumulate(way, owner):
+        lanes = slice(way * half, (way + 1) * half)
+        grad_sum[:, lanes] += dot_last(cotangent[owner], weight[owner, lanes, :])
+
+    for way in range(2):
+        accumulate(way, me)
+
+    def pump(step, last):
+        for way in range(2):
+            ring(way, step).wait()
+            if not last:
+                ring(way, step + 1).start()
+        for way in range(2):
+            accumulate(way, at_place(place - (1 - 2 * way) * (step + 1)))
+
+    def early(step, _):
+        pump(step, False)
+        return 0
+
+    lax.fori_loop(0, 2, early, 0)
+    for j in range(1, parts):
+        for copy in token_copies(j):
+            copy.wait()
+    cluster_places(ids_in, rows, parts, places, place_cols)
+
+    def read_part(part):
+        return jnp.concatenate([q_in[part], k_in[part], v_in[part]], axis=1)
+
+    def attend_cluster(cluster):
+        picked = to_cluster(places, rows, parts, cluster, read_part)
+        ordered[cluster] = picked
+        query, key, value = (picked[:, i * HD : (i + 1) * HD] for i in range(3))
+        probs = cluster_probs(pattern_ref, cluster, query, key, rows, score_scale)
+        probs_at[cluster] = probs
+        at = pl.multiple_of(cluster * rows, rows)
+        held[pl.ds(at, rows), :] = dot_rows(probs.astype(jnp.bfloat16), value).astype(jnp.bfloat16)
+
+    def middle(step, _):
+        pump(step, False)
+        attend_cluster(2 * (step - 2))
+        attend_cluster(2 * (step - 2) + 1)
+        return 0
+
+    lax.fori_loop(2, 2 + line, middle, 0)
+    for part in range(parts):
+        mixed_send[part] = from_clusters(place_cols, rows, parts, part, held[...])
+
+    def attn_copy(j):
+        return along_seq(4, j, mixed_send.at[other(j)], attn.at[:, head_at(me)])
+
+    for j in range(1, parts):
+        attn_copy(j).start()
+    attn[:, head_at(me)] = mixed_send[me]
+
+    pump(parts - 2, True)
+    for part in range(parts):
+        grad_send[part] = grad_sum[:, part * HD : (part + 1) * HD].astype(jnp.bfloat16)
+
+    def grad_copy(j):
+        return along_seq(5, j, grad_send.at[other(j)], grad_in.at[me])
+
+    for j in range(1, parts):
+        grad_copy(j).start()
+    grad_in[me] = grad_send[me]
+
+    for j in range(1, parts):
+        attn_copy(j).wait()
+
+    def project(owner, _):
+        partial[owner] = dot_rows(attn[...], weight[owner]).astype(jnp.bfloat16)
+        return 0
+
+    lax.fori_loop(0, parts, project, 0)
+
+    def share_copy(j):
+        return along_head(1, j, partial.at[pl.ds(2 * other_group(j), 2)], shares.at[group])
+
+    for j in range(1, groups):
+        share_copy(j).start()
+    shares[group] = partial[pl.ds(2 * group, 2)]
+
+    for j in range(1, parts):
+        grad_copy(j).wait()
+
+    def back_values(cluster, _):
+        grad = to_cluster(places, rows, parts, cluster, lambda part: grad_in[part])
+        value = ordered[cluster, :, 2 * HD : 3 * HD]
+        probs = probs_at[cluster]
+        here = pl.ds(pl.multiple_of(cluster * rows, rows), rows)
+        delta = jnp.sum(
+            grad.astype(jnp.float32) * held[here, :].astype(jnp.float32), axis=1, keepdims=True
+        )
+        dscores_at[cluster] = (probs * (dot_last(grad, value) - delta)).astype(jnp.bfloat16)
+        held_v[here, :] = dot_first(probs.astype(jnp.bfloat16), grad).astype(jnp.bfloat16)
+        return 0
+
+    lax.fori_loop(0, parts, back_values, 0, unroll=2)
+    for part in range(parts):
+        back_v[part] = from_clusters(place_cols, rows, parts, part, held_v[...])
+
+    def value_copy(j):
+        return along_seq(6, j, back_v.at[other(j)], gv_ref.at[:, head_at(me)])
+
+    for j in range(1, parts):
+        value_copy(j).start()
+    gv_ref[:, head_at(me)] = back_v[me]
+
+    def back_scores(cluster, _):
+        query, key = (ordered[cluster, :, i * HD : (i + 1) * HD] for i in range(2))
+        dscores = dscores_at[cluster]
+        here = pl.ds(pl.multiple_of(cluster * rows, rows), rows)
+        held_qk[here, 0:HD] = (dot_rows(dscores, key) * score_scale).astype(jnp.bfloat16)
+        held_qk[here, HD:] = (dot_first(dscores, query) * score_scale).astype(jnp.bfloat16)
+        return 0
+
+    lax.fori_loop(0, parts, back_scores, 0, unroll=2)
+    for part in range(parts):
+        back = from_clusters(place_cols, rows, parts, part, held_qk[...])
+        back_q[part] = back[:, :HD]
+        back_k[part] = back[:, HD:]
+
+    def pair_copies(j):
+        return (
+            along_seq(7, j, back_q.at[other(j)], gq_ref.at[:, head_at(me)]),
+            along_seq(8, j, back_k.at[other(j)], gk_ref.at[:, head_at(me)]),
+        )
+
+    for j in range(1, parts):
+        for copy in pair_copies(j):
+            copy.start()
+    gq_ref[:, head_at(me)] = back_q[me]
+    gk_ref[:, head_at(me)] = back_k[me]
+
+    for j in range(1, groups):
+        share_copy(j).wait()
+    for i in range(2):
+        total = shares[0, i].astype(jnp.float32)
+        for j in range(1, groups):
+            total = total + shares[j, i].astype(jnp.float32)
+        out_ref[:, i * cols : (i + 1) * cols] = total.astype(jnp.bfloat16)
+
+    for j in range(1, parts):
+        value_copy(j).wait()
+        for copy in pair_copies(j):
+            copy.wait()
+
+
+VMEM_SPEC = pl.BlockSpec(memory_space=pltpu.VMEM)
+SMEM_SPEC = pl.BlockSpec(memory_space=pltpu.SMEM)
+
+
+def by_heads(queries, key_rows, value_rows, out_weight, grad_output, cluster_ids, block_pattern):
+    rows, width = queries.shape
+    parts = lax.axis_size("seq")
+    groups = lax.axis_size("head")
+    depth, cols = out_weight.shape
+    id_rows = jnp.pad(
+        cluster_ids.reshape(-1, HD).astype(jnp.bfloat16), ((0, ID_ROWS - rows // HD), (0, 0))
+    )
+    low, full = jnp.bfloat16, jnp.float32
+
+    def vmem(*shape, kind=low):
+        return pltpu.VMEM(shape, kind)
+
+    scratch = [
+        vmem(parts, rows, HD), vmem(parts, rows, HD), vmem(parts, rows, HD),
+        vmem(parts, ID_ROWS, HD), vmem(parts, depth, cols), vmem(parts, rows, cols),
+        vmem(parts, rows, kind=full), vmem(rows, HD, kind=full), vmem(parts, rows, 3 * HD),
+        vmem(parts, rows, rows, kind=full), vmem(parts * rows, HD), vmem(parts, rows, HD),
+        vmem(rows, width), vmem(rows, width, kind=full), vmem(parts, rows, HD),
+        vmem(parts, rows, HD), vmem(parts, rows, rows), vmem(parts * rows, 2 * HD),
+        vmem(parts * rows, HD), vmem(parts, rows, HD), vmem(parts, rows, HD), vmem(parts, rows, HD),
+        vmem(parts, rows, cols), vmem(groups, 2, rows, cols),
+        pltpu.SemaphoreType.DMA((9, parts)), pltpu.SemaphoreType.DMA((9, parts)),
+        pltpu.SemaphoreType.DMA((2, parts)), pltpu.SemaphoreType.DMA((2, parts)),
+        pltpu.SemaphoreType.DMA((2, groups)), pltpu.SemaphoreType.DMA((2, groups)),
+        pltpu.SemaphoreType.DMA((1,)),
+    ]
+    return pl.pallas_call(
+        functools.partial(layer_kernel, rows, parts, groups),
+        out_shape=(jax.ShapeDtypeStruct((rows, width), low),) * 4,
+        in_specs=[SMEM_SPEC] + [VMEM_SPEC] * 6,
+        out_specs=(VMEM_SPEC,) * 4,
+        scratch_shapes=scratch,
+        compiler_params=pltpu.CompilerParams(
+            collective_id=0, has_side_effects=True, vmem_limit_bytes=56 * 1024 * 1024
+        ),
+        name="routing_layer",
+    )(block_pattern.reshape(-1), id_rows, queries, key_rows, value_rows, out_weight, grad_output)
+
+
+def on_device(queries, *others):
+    heads = queries.shape[1] // HD
+    parts, groups = lax.axis_size("seq"), lax.axis_size("head")
+    if heads == parts == 2 * groups and others[-1].shape[1] == 2:
+        return by_heads(queries, *others)
+    return by_clusters(queries, *others)
+
+
 def solution(mesh):
     in_specs = (
         P("seq", "head"),

time: 412 us -> 193 us (0.47); the launches traced: 405 us -> 192 us
  Pallas kernels: 0 us -> 184 us
  waiting for transfers between devices: 166 us -> 0 us
  matrix products: 95.2 us -> 0 us
  starting transfers between devices: 57.3 us -> 0 us
  local copies, waits for them, and re-layouts: 43.7 us -> 6.57 us
  other arithmetic: 28.9 us -> 0.68 us
  between operations: 14.3 us -> 0.65 us
    pallas_call x0 -> x1, Pallas kernels: none -> 184 us  [by_heads(): pl.pallas_call(functools.partial(layer_kernel, rows, parts, groups), out_...]
    all_to_all x9 -> x0, waiting for transfers between devices: 145 us -> none  [the longest x1 47.3 us: on_device(): lax.all_to_all(to_slots(value_rows), 'seq', split_axis=0, concat_axis=0,...]
    dot_general x51 -> x0, matrix products: 95.2 us -> none  [the longest x8 17.2 us: attend_back(): jnp.einsum('qd,kd->qk', grad_head, value_head, preferred_element_type=jnp...]
    all_to_all x9 -> x0, starting transfers between devices: 57.2 us -> none  [the longest x1 7.28 us: on_device(): lax.all_to_all(attn_side, 'seq', split_axis=0, concat_axis=0, tiled=True)]
    all_gather x2 -> x0, waiting for transfers between devices: 19.6 us -> none  [the longest x1 19.6 us: on_device(): full_weight = lax.all_gather(out_weight, 'seq', axis=1, tiled=True)]
    scatter x4 -> x0, local copies, waits for them, and re-layouts: 12.1 us -> none  [to_slots(): jnp.zeros((slot_total, row_data.shape[1]), row_data.dtype).at[slot_index]]
    concatenate x4 -> x0, local copies, waits for them, and re-layouts: 9.14 us -> none  [the longest x1 2.29 us: attend(): return jnp.concatenate(results, axis=1)]
    reduce_sum x17 -> x0, other arithmetic: 8.52 us -> none  [the longest x8 6.07 us: attend_back(): jnp.sum(grad_head.astype(jnp.float32) * attn_head.astype(jnp.float32), ax...]
  transfers between devices with their start and end apart: 12 -> 0, of which waited for: 8 -> 0; matrix products, arithmetic and copies ran while one was open for 41% -> 0% of each run, Pallas kernels for 0% -> 0%
where the time goes in v2:
time: 193 us; the launch traced here: 192 us
  Pallas kernels  184 us (95%)
  local copies, waits for them, and re-layouts  6.57 us (3%)
    pallas_call x1, Pallas kernels, by_heads(): pl.pallas_call(functools.partial(layer_kernel, rows, parts, groups), out_...  184 us
    unnamed x13, local copies, waits for them, and re-layouts  5.36 us

profile of v2, /device:TPU:28, one launch (start us, length us, event | category | flops | bytes accessed | tf_op | source)
XLA Modules:
  0.0 192.2 jit_solution(8312307734767856122)
XLA Ops:
  0.6 0.7 convert_bitcast_fusion
  1.3 0.0 copy-start.3
  1.3 0.6 pad.4.ids_ref
  1.9 0.1 copy-done.3
  2.0 0.1 copy.12
  2.1 0.6 reshape.13.pattern_ref
  2.7 184.3 %routing_layer.1 = (bf16[256,1024]{1,0:T(8,128)(2,1)}, bf16[256,1024]{1,0:T(8,128)(2,1)}, bf16[256,1024]{1,0:T(8,128)(2,1)}, bf16[256,1024]{1,0:T(8,128)(2,1)}) custom-call(s32[32]{0:T(128)} %reshape.13.pattern_ref, bf16[16,128]{1,0:T(8,128)(2,1)} %pad.4.ids_ref, bf16[256,1024]{1,0:T(8,128)(2,1)} %q_ref.1, bf16[256,1024]{1,0:T(8,128)(2,1)} %k_ref.1, ...), custom_call_target="tpu_custom_call" | custom-call | tf_op jit(solution)/shard_map/routing_layer/pallas_call | solution.py:523
  187.0 0.0 copy-start.2
  187.0 1.9 %copy.17 = bf16[256,1024]{1,0:T(8,128)(2,1)} copy(bf16[256,1024]{1,0:T(8,128)(2,1)} %get-tuple-element.8) | data formatting | bytes 1048576
  189.0 0.0 copy-done.2
  189.0 0.0 copy-start.1
  189.0 0.8 copy.18
  189.8 0.4 copy-done.1
  190.2 0.0 copy-start
  190.2 0.8 copy.19
  191.0 0.4 copy-done
  191.4 0.8 copy.20
Async XLA Ops:
  1.3 0.7 copy-start.3
  187.0 1.9 %copy-start.2 = (bf16[256,1024]{1,0:T(8,128)(2,1)S(1)}, bf16[256,1024]{1,0:T(8,128)(2,1)}, u32[]{:S(2)}) copy-start(bf16[256,1024]{1,0:T(8,128)(2,1)} %get-tuple-element.9) | copy-start | bytes 1572868
  189.0 1.2 copy-start.1
  190.2 1.2 copy-start

commit v3 on v2

--- a/solution.py
+++ b/solution.py
@@ -164,6 +164,7 @@
 
 
 ID_ROWS = 16
+EARLY = 6
 MESH = pl.DeviceIdType.MESH
 
 
@@ -256,6 +257,8 @@
     me = lax.axis_index("seq")
     group = lax.axis_index("head")
     half = w_ref.shape[0] // 2
+    quarter = half // 2
+    ticks = 2 * (parts - 1)
     cols = w_ref.shape[1]
 
     def other(j):
@@ -288,12 +291,13 @@
         far = p // line
         return 2 * (p + far * (parts - 1 - 2 * p)) + far
 
-    def ring(way, step):
+    def ring(way, tick):
         sign = 1 - 2 * way
-        block = weight.at[at_place(place - sign * step), pl.ds(way * half, half)]
+        at = pl.multiple_of(way * half + lax.rem(tick, 2) * quarter, quarter)
+        block = weight.at[at_place(place - sign * (tick // 2)), pl.ds(at, quarter)]
         return pltpu.make_async_remote_copy(
-            src_ref=block, dst_ref=block, send_sem=ring_send.at[way, step],
-            recv_sem=ring_recv.at[way, step], device_id={"seq": at_place(place + sign)},
+            src_ref=block, dst_ref=block, send_sem=ring_send.at[way, tick],
+            recv_sem=ring_recv.at[way, tick], device_id={"seq": at_place(place + sign)},
             device_id_type=MESH,
         )
 
@@ -310,8 +314,9 @@
     pl.semaphore_wait(barrier, parts + groups - 2)
 
     own_weight.wait()
-    for way in range(2):
-        ring(way, 0).start()
+    for tick in range(2):
+        for way in range(2):
+            ring(way, jnp.int32(tick)).start()
 
     def head_copies(j):
         block = cotangent.at[pl.ds(2 * group, 2)]
@@ -337,31 +342,42 @@
     v_in[me] = v_ref[:, head_at(me)]
     ids_in[me] = ids_ref[...]
 
-    grad_sum[...] = jnp.zeros_like(grad_sum)
-
+    def forward(tick):
+        for way in range(2):
+            ring(way, tick).wait_recv()
+
+            @pl.when(tick + 2 < ticks)
+            def _():
+                ring(way, tick + 2).start()
+
+    def accumulate(tick):
+        for way in range(2):
+            owner = at_place(place - (1 - 2 * way) * (tick // 2 + 1))
+            at = pl.multiple_of(way * half + lax.rem(tick, 2) * quarter, quarter)
+            here = pl.ds(at, quarter)
+            grad_sum[:, here] += dot_last(cotangent[owner], weight[owner, here, :])
+
+    def pass_on(tick, _):
+        forward(tick)
+        return 0
+
+    def add_up(tick, _):
+        accumulate(tick)
+        return 0
+
+    def pump(tick, _):
+        forward(tick)
+        accumulate(tick)
+        return 0
+
+    lax.fori_loop(0, 2, pass_on, 0)
     for j in range(1, groups):
         head_copies(j).wait()
-
-    def accumulate(way, owner):
-        lanes = slice(way * half, (way + 1) * half)
-        grad_sum[:, lanes] += dot_last(cotangent[owner], weight[owner, lanes, :])
-
-    for way in range(2):
-        accumulate(way, me)
-
-    def pump(step, last):
-        for way in range(2):
-            ring(way, step).wait()
-            if not last:
-                ring(way, step + 1).start()
-        for way in range(2):
-            accumulate(way, at_place(place - (1 - 2 * way) * (step + 1)))
-
-    def early(step, _):
-        pump(step, False)
-        return 0
-
-    lax.fori_loop(0, 2, early, 0)
+    for i in range(4):
+        lanes = slice(i * quarter, (i + 1) * quarter)
+        grad_sum[:, lanes] = dot_last(cotangent[me], weight[me, lanes, :])
+    lax.fori_loop(0, 2, add_up, 0)
+    lax.fori_loop(2, EARLY, pump, 0)
     for j in range(1, parts):
         for copy in token_copies(j):
             copy.wait()
@@ -379,49 +395,32 @@
         at = pl.multiple_of(cluster * rows, rows)
         held[pl.ds(at, rows), :] = dot_rows(probs.astype(jnp.bfloat16), value).astype(jnp.bfloat16)
 
-    def middle(step, _):
-        pump(step, False)
-        attend_cluster(2 * (step - 2))
-        attend_cluster(2 * (step - 2) + 1)
-        return 0
-
-    lax.fori_loop(2, 2 + line, middle, 0)
+    def middle(tick, _):
+        pump(tick, 0)
+        attend_cluster(tick - EARLY)
+        return 0
+
+    lax.fori_loop(EARLY, EARLY + parts - 1, middle, 0)
+    attend_cluster(jnp.int32(parts - 1))
+    lax.fori_loop(EARLY + parts - 1, ticks, pump, 0)
+    def attn_copy(j):
+        return along_seq(4, j, mixed_send.at[other(j)], attn.at[:, head_at(me)])
+
+    for part in range(parts):
+        grad_send[part] = grad_sum[:, part * HD : (part + 1) * HD].astype(jnp.bfloat16)
+
+    def grad_copy(j):
+        return along_seq(5, j, grad_send.at[other(j)], grad_in.at[me])
+
+    for j in range(1, parts):
+        grad_copy(j).start()
+    grad_in[me] = grad_send[me]
+
     for part in range(parts):
         mixed_send[part] = from_clusters(place_cols, rows, parts, part, held[...])
-
-    def attn_copy(j):
-        return along_seq(4, j, mixed_send.at[other(j)], attn.at[:, head_at(me)])
-
     for j in range(1, parts):
         attn_copy(j).start()
     attn[:, head_at(me)] = mixed_send[me]
-
-    pump(parts - 2, True)
-    for part in range(parts):
-        grad_send[part] = grad_sum[:, part * HD : (part + 1) * HD].astype(jnp.bfloat16)
-
-    def grad_copy(j):
-        return along_seq(5, j, grad_send.at[other(j)], grad_in.at[me])
-
-    for j in range(1, parts):
-        grad_copy(j).start()
-    grad_in[me] = grad_send[me]
-
-    for j in range(1, parts):
-        attn_copy(j).wait()
-
-    def project(owner, _):
-        partial[owner] = dot_rows(attn[...], weight[owner]).astype(jnp.bfloat16)
-        return 0
-
-    lax.fori_loop(0, parts, project, 0)
-
-    def share_copy(j):
-        return along_head(1, j, partial.at[pl.ds(2 * other_group(j), 2)], shares.at[group])
-
-    for j in range(1, groups):
-        share_copy(j).start()
-    shares[group] = partial[pl.ds(2 * group, 2)]
 
     for j in range(1, parts):
         grad_copy(j).wait()
@@ -475,6 +474,22 @@
     gq_ref[:, head_at(me)] = back_q[me]
     gk_ref[:, head_at(me)] = back_k[me]
 
+    for j in range(1, parts):
+        attn_copy(j).wait()
+
+    def project(owner, _):
+        partial[owner] = dot_rows(attn[...], weight[owner]).astype(jnp.bfloat16)
+        return 0
+
+    lax.fori_loop(0, parts, project, 0)
+
+    def share_copy(j):
+        return along_head(1, j, partial.at[pl.ds(2 * other_group(j), 2)], shares.at[group])
+
+    for j in range(1, groups):
+        share_copy(j).start()
+    shares[group] = partial[pl.ds(2 * group, 2)]
+
     for j in range(1, groups):
         share_copy(j).wait()
     for i in range(2):
@@ -487,6 +502,13 @@
         value_copy(j).wait()
         for copy in pair_copies(j):
             copy.wait()
+
+    def sent(tick, _):
+        for way in range(2):
+            ring(way, tick).wait_send()
+        return 0
+
+    lax.fori_loop(0, ticks, sent, 0)
 
 
 VMEM_SPEC = pl.BlockSpec(memory_space=pltpu.VMEM)
@@ -516,7 +538,7 @@
         vmem(parts * rows, HD), vmem(parts, rows, HD), vmem(parts, rows, HD), vmem(parts, rows, HD),
         vmem(parts, rows, cols), vmem(groups, 2, rows, cols),
         pltpu.SemaphoreType.DMA((9, parts)), pltpu.SemaphoreType.DMA((9, parts)),
-        pltpu.SemaphoreType.DMA((2, parts)), pltpu.SemaphoreType.DMA((2, parts)),
+        pltpu.SemaphoreType.DMA((2, 2 * parts)), pltpu.SemaphoreType.DMA((2, 2 * parts)),
         pltpu.SemaphoreType.DMA((2, groups)), pltpu.SemaphoreType.DMA((2, groups)),
         pltpu.SemaphoreType.DMA((1,)),
     ]

time: 193 us -> 190 us (0.984)
  Pallas kernels: 184 us -> 181 us
    pallas_call x1, Pallas kernels: 184 us -> 181 us  [by_heads(): pl.pallas_call(functools.partial(layer_kernel, rows, parts, groups), out_...]
where the time goes in v3:
time: 190 us; the launch traced here: 189 us
  Pallas kernels  181 us (95%)
  local copies, waits for them, and re-layouts  6.57 us (3%)
    pallas_call x1, Pallas kernels, by_heads(): pl.pallas_call(functools.partial(layer_kernel, rows, parts, groups), out_...  181 us
    unnamed x13, local copies, waits for them, and re-layouts  5.36 us

profile of v3, /device:TPU:28, one launch (start us, length us, event | category | flops | bytes accessed | tf_op | source)
XLA Modules:
  0.0 189.3 jit_solution(6928086389059511469)
XLA Ops:
  0.6 0.7 convert_bitcast_fusion
  1.3 0.0 copy-start.3
  1.3 0.6 pad.4.ids_ref
  1.9 0.1 copy-done.3
  2.0 0.1 copy.12
  2.1 0.6 reshape.13.pattern_ref
  2.7 181.3 %routing_layer.1 = (bf16[256,1024]{1,0:T(8,128)(2,1)}, bf16[256,1024]{1,0:T(8,128)(2,1)}, bf16[256,1024]{1,0:T(8,128)(2,1)}, bf16[256,1024]{1,0:T(8,128)(2,1)}) custom-call(s32[32]{0:T(128)} %reshape.13.pattern_ref, bf16[16,128]{1,0:T(8,128)(2,1)} %pad.4.ids_ref, bf16[256,1024]{1,0:T(8,128)(2,1)} %q_ref.1, bf16[256,1024]{1,0:T(8,128)(2,1)} %k_ref.1, ...), custom_call_target="tpu_custom_call" | custom-call | tf_op jit(solution)/shard_map/routing_layer/pallas_call | solution.py:545
  184.1 0.0 copy-start.2
  184.1 1.9 %copy.17 = bf16[256,1024]{1,0:T(8,128)(2,1)} copy(bf16[256,1024]{1,0:T(8,128)(2,1)} %get-tuple-element.8) | data formatting | bytes 1048576
  186.0 0.0 copy-done.2
  186.0 0.0 copy-start.1
  186.0 0.8 copy.18
  186.8 0.4 copy-done.1
  187.2 0.0 copy-start
  187.2 0.8 copy.19
  188.0 0.4 copy-done
  188.5 0.8 copy.20
Async XLA Ops:
  1.3 0.7 copy-start.3
  184.1 1.9 %copy-start.2 = (bf16[256,1024]{1,0:T(8,128)(2,1)S(1)}, bf16[256,1024]{1,0:T(8,128)(2,1)}, u32[]{:S(2)}) copy-start(bf16[256,1024]{1,0:T(8,128)(2,1)} %get-tuple-element.9) | copy-start | bytes 1572868
  186.0 1.2 copy-start.1
  187.2 1.2 copy-start

commit v4 on v3

--- a/solution.py
+++ b/solution.py
@@ -164,7 +164,6 @@
 
 
 ID_ROWS = 16
-EARLY = 6
 MESH = pl.DeviceIdType.MESH
 
 
@@ -251,14 +250,15 @@
     q_in, k_in, v_in, ids_in, weight, cotangent, places, place_cols, ordered, probs_at, held,
     mixed_send, attn, grad_sum, grad_send, grad_in, dscores_at, held_qk, held_v, back_q, back_k, back_v,
     partial, shares,
-    tok_send, tok_recv, ring_send, ring_recv, head_send, head_recv, own_sem,
+    tok_send, tok_recv, ring_send, ring_recv, hop_send, hop_recv, across_send, across_recv, head_send, head_recv, own_sem,
 ):
     score_scale = 1.0 / math.sqrt(HD)
     me = lax.axis_index("seq")
     group = lax.axis_index("head")
     half = w_ref.shape[0] // 2
     quarter = half // 2
-    ticks = 2 * (parts - 1)
+    ticks = parts - 1
+    lower = pl.ds(half, half)
     cols = w_ref.shape[1]
 
     def other(j):
@@ -293,14 +293,39 @@
 
     def ring(way, tick):
         sign = 1 - 2 * way
-        at = pl.multiple_of(way * half + lax.rem(tick, 2) * quarter, quarter)
-        block = weight.at[at_place(place - sign * (tick // 2)), pl.ds(at, quarter)]
+        block = weight.at[at_place(place - sign * tick), pl.ds(way * quarter, quarter)]
         return pltpu.make_async_remote_copy(
             src_ref=block, dst_ref=block, send_sem=ring_send.at[way, tick],
             recv_sem=ring_recv.at[way, tick], device_id={"seq": at_place(place + sign)},
             device_id_type=MESH,
         )
 
+    def hop(way, k):
+        sign = 1 - 2 * way
+        block = weight.at[2 * lax.rem(row - sign * k + line, line) + side, lower]
+        return pltpu.make_async_remote_copy(
+            src_ref=block, dst_ref=block, send_sem=hop_send.at[way, k],
+            recv_sem=hop_recv.at[way, k],
+            device_id={"seq": 2 * lax.rem(row + sign + line, line) + side}, device_id_type=MESH,
+        )
+
+    def hop_goes(way, k):
+        return (row >= k) & (row < line - 1) if way == 0 else (row + k < line) & (row > 0)
+
+    def hop_comes(way, k):
+        return row >= k + 1 if way == 0 else row + k + 1 < line
+
+    def hop_owner(way, k):
+        return lax.rem(row - (1 - 2 * way) * (k + 1) + line, line)
+
+    def across(level):
+        block = weight.at[2 * level + side, lower]
+        return pltpu.make_async_remote_copy(
+            src_ref=block, dst_ref=block, send_sem=across_send.at[level],
+            recv_sem=across_recv.at[level], device_id={"seq": 2 * row + 1 - side},
+            device_id_type=MESH,
+        )
+
     own_weight = pltpu.make_async_copy(w_ref, weight.at[me], own_sem.at[0])
     own_weight.start()
     for i in range(2):
@@ -314,9 +339,15 @@
     pl.semaphore_wait(barrier, parts + groups - 2)
 
     own_weight.wait()
-    for tick in range(2):
-        for way in range(2):
-            ring(way, jnp.int32(tick)).start()
+    def start_hop(way, k):
+        @pl.when(hop_goes(way, k))
+        def _():
+            hop(way, k).start()
+
+    for way in range(2):
+        ring(way, jnp.int32(0)).start()
+        start_hop(way, 0)
+    across(row).start()
 
     def head_copies(j):
         block = cotangent.at[pl.ds(2 * group, 2)]
@@ -346,38 +377,49 @@
         for way in range(2):
             ring(way, tick).wait_recv()
 
-            @pl.when(tick + 2 < ticks)
+            @pl.when(tick + 1 < ticks)
             def _():
-                ring(way, tick + 2).start()
+                ring(way, tick + 1).start()
 
     def accumulate(tick):
         for way in range(2):
-            owner = at_place(place - (1 - 2 * way) * (tick // 2 + 1))
-            at = pl.multiple_of(way * half + lax.rem(tick, 2) * quarter, quarter)
-            here = pl.ds(at, quarter)
+            owner = at_place(place - (1 - 2 * way) * (tick + 1))
+            here = slice(way * quarter, (way + 1) * quarter)
             grad_sum[:, here] += dot_last(cotangent[owner], weight[owner, here, :])
 
-    def pass_on(tick, _):
-        forward(tick)
-        return 0
-
-    def add_up(tick, _):
-        accumulate(tick)
-        return 0
-
-    def pump(tick, _):
-        forward(tick)
-        accumulate(tick)
-        return 0
-
-    lax.fori_loop(0, 2, pass_on, 0)
+    def add_lower(owner):
+        grad_sum[:, half:] += dot_last(cotangent[owner], weight[owner, half:, :])
+
+    def receive_hops(k):
+        for way in range(2):
+
+            @pl.when(hop_comes(way, k))
+            def _(way=way):
+                hop(way, k).wait_recv()
+                if k + 1 < line - 1:
+                    start_hop(way, k + 1)
+                across(hop_owner(way, k)).start()
+
+        for way in range(2):
+
+            @pl.when(hop_comes(way, k))
+            def _(way=way):
+                add_lower(2 * hop_owner(way, k) + side)
+
+    def pump(tick):
+        forward(jnp.int32(tick))
+        accumulate(jnp.int32(tick))
+
+    forward(jnp.int32(0))
     for j in range(1, groups):
         head_copies(j).wait()
     for i in range(4):
         lanes = slice(i * quarter, (i + 1) * quarter)
         grad_sum[:, lanes] = dot_last(cotangent[me], weight[me, lanes, :])
-    lax.fori_loop(0, 2, add_up, 0)
-    lax.fori_loop(2, EARLY, pump, 0)
+    accumulate(jnp.int32(0))
+    pump(1)
+    receive_hops(0)
+    pump(2)
     for j in range(1, parts):
         for copy in token_copies(j):
             copy.wait()
@@ -395,14 +437,23 @@
         at = pl.multiple_of(cluster * rows, rows)
         held[pl.ds(at, rows), :] = dot_rows(probs.astype(jnp.bfloat16), value).astype(jnp.bfloat16)
 
-    def middle(tick, _):
-        pump(tick, 0)
-        attend_cluster(tick - EARLY)
-        return 0
-
-    lax.fori_loop(EARLY, EARLY + parts - 1, middle, 0)
-    attend_cluster(jnp.int32(parts - 1))
-    lax.fori_loop(EARLY + parts - 1, ticks, pump, 0)
+    def attend_some(first, count):
+        def some(cluster, _):
+            attend_cluster(cluster)
+            return 0
+
+        lax.fori_loop(first, first + count, some, 0)
+
+    share = parts // line
+    for k in range(1, line - 1):
+        pump(2 * k + 1)
+        attend_some((2 * k - 2) * share, share)
+        receive_hops(k)
+        pump(2 * k + 2)
+        attend_some((2 * k - 1) * share, share)
+    for level in range(line):
+        across(level).wait_recv()
+        add_lower(2 * level + 1 - side)
     def attn_copy(j):
         return along_seq(4, j, mixed_send.at[other(j)], attn.at[:, head_at(me)])
 
@@ -509,6 +560,15 @@
         return 0
 
     lax.fori_loop(0, ticks, sent, 0)
+    for k in range(line - 1):
+        for way in range(2):
+
+            @pl.when(hop_goes(way, k))
+            def _(way=way, k=k):
+                hop(way, k).wait_send()
+
+    for level in range(line):
+        across(level).wait_send()
 
 
 VMEM_SPEC = pl.BlockSpec(memory_space=pltpu.VMEM)
@@ -538,7 +598,9 @@
         vmem(parts * rows, HD), vmem(parts, rows, HD), vmem(parts, rows, HD), vmem(parts, rows, HD),
         vmem(parts, rows, cols), vmem(groups, 2, rows, cols),
         pltpu.SemaphoreType.DMA((9, parts)), pltpu.SemaphoreType.DMA((9, parts)),
-        pltpu.SemaphoreType.DMA((2, 2 * parts)), pltpu.SemaphoreType.DMA((2, 2 * parts)),
+        pltpu.SemaphoreType.DMA((2, parts)), pltpu.SemaphoreType.DMA((2, parts)),
+        pltpu.SemaphoreType.DMA((2, parts)), pltpu.SemaphoreType.DMA((2, parts)),
+        pltpu.SemaphoreType.DMA((parts,)), pltpu.SemaphoreType.DMA((parts,)),
         pltpu.SemaphoreType.DMA((2, groups)), pltpu.SemaphoreType.DMA((2, groups)),
         pltpu.SemaphoreType.DMA((1,)),
     ]

time: 190 us -> 191 us (level)
  Pallas kernels: 181 us -> 183 us
where the time goes in v4:
time: 191 us
  Pallas kernels  183 us (96%)
  local copies, waits for them, and re-layouts  6.57 us (3%)
    pallas_call x1, Pallas kernels, by_heads(): pl.pallas_call(functools.partial(layer_kernel, rows, parts, groups), out_...  183 us
    unnamed x13, local copies, waits for them, and re-layouts  5.36 us

profile of v4, /device:TPU:28, one launch (start us, length us, event | category | flops | bytes accessed | tf_op | source)
XLA Modules:
  0.0 190.8 jit_solution(9342980983546866327)
XLA Ops:
  0.6 0.7 convert_bitcast_fusion
  1.3 0.0 copy-start.3
  1.3 0.6 pad.4.ids_ref
  1.9 0.1 copy-done.3
  2.0 0.1 copy.12
  2.1 0.6 reshape.13.pattern_ref
  2.7 182.9 %routing_layer.1 = (bf16[256,1024]{1,0:T(8,128)(2,1)}, bf16[256,1024]{1,0:T(8,128)(2,1)}, bf16[256,1024]{1,0:T(8,128)(2,1)}, bf16[256,1024]{1,0:T(8,128)(2,1)}) custom-call(s32[32]{0:T(128)} %reshape.13.pattern_ref, bf16[16,128]{1,0:T(8,128)(2,1)} %pad.4.ids_ref, bf16[256,1024]{1,0:T(8,128)(2,1)} %q_ref.1, bf16[256,1024]{1,0:T(8,128)(2,1)} %k_ref.1, ...), custom_call_target="tpu_custom_call" | custom-call | tf_op jit(solution)/shard_map/routing_layer/pallas_call | solution.py:607
  185.6 0.0 copy-start.2
  185.7 1.9 %copy.17 = bf16[256,1024]{1,0:T(8,128)(2,1)} copy(bf16[256,1024]{1,0:T(8,128)(2,1)} %get-tuple-element.8) | data formatting | bytes 1048576
  187.6 0.0 copy-done.2
  187.6 0.0 copy-start.1
  187.6 0.8 copy.18
  188.4 0.4 copy-done.1
  188.8 0.0 copy-start
  188.8 0.8 copy.19
  189.6 0.4 copy-done
  190.1 0.8 copy.20
Async XLA Ops:
  1.3 0.7 copy-start.3
  185.6 1.9 %copy-start.2 = (bf16[256,1024]{1,0:T(8,128)(2,1)S(1)}, bf16[256,1024]{1,0:T(8,128)(2,1)}, u32[]{:S(2)}) copy-start(bf16[256,1024]{1,0:T(8,128)(2,1)} %get-tuple-element.9) | copy-start | bytes 1572868
  187.6 1.2 copy-start.1
  188.8 1.2 copy-start
